TPU v7x, 32 devices: a whole 2x2x4 slice. The times are simulated.
32 devices in a mesh: row: 4 (over z), col: 8 (over y, x, core).
Axes of the slice: x: 2, y: 2, z: 4, core: 2. Of those that a mesh axis runs over, the one named last changes fastest.
Arguments:
- tokens: bfloat16 [2560, 8192], P('row', 'col'), may hold values from -6 to 6
- norm_gain: bfloat16 [8192], replicated, may hold values from 0.099609375 to 1.8984375
- w_query: bfloat16 [8192, 8192], P('row', 'col')
- w_key: bfloat16 [8192, 1024], P('row')
- w_value: bfloat16 [8192, 1024], P('row'), may hold values from -0.0625 to 0.0625
- w_out: bfloat16 [8192, 8192], P('row', 'col'), may hold values from -0.0625 to 0.0625
- doc_lengths: int32 [4], replicated, may hold values from 1 to 1280, 2560 in all
Outputs:
- layer_out: bfloat16 [2560, 8192], P('row', 'col')
Inputs may be any that keep to these rules, and one draw needn't show every extreme that they name: `doc_lengths`: positive lengths that add up to 2560; the largest is exactly 1280.
All inputs are finite; a program needn't handle non-finite values.
Results may differ from a plain program's by a relative error of at most 0.011.
Values may be sent and summed in bfloat16 or wider, within the bound.
No kernel may reach another device: no remote copies, remote signals or barrier semaphores. Data moves between devices by JAX's collectives and lax.ppermute only.
A program may use at most 192 MiB of HBM per device.

v0:
```python
import jax
import jax.numpy as jnp
from jax import lax
from jax.sharding import PartitionSpec as P

HEADS = 64
KVH = 8
HD = 128
rope_base = 500000.0
norm_eps = 1e-05
masked_value = -1e30


def rope_tables(positions, head_dim):
    freq_index = jnp.arange(head_dim // 2, dtype=jnp.int32).astype(jnp.float32)
    inverse = rope_base ** (-2.0 * freq_index / head_dim)
    angles = positions.astype(jnp.float32)[:, None] * inverse[None, :]
    return (jnp.cos(angles), jnp.sin(angles))


def rotate(vectors, cosine, sine):
    half_dim = vectors.shape[-1] // 2
    first = vectors[..., :half_dim]
    second = vectors[..., half_dim:]
    cos_part = cosine[:, None, :]
    sin_part = sine[:, None, :]
    return jnp.concatenate(
        [first * cos_part - second * sin_part, second * cos_part + first * sin_part], axis=-1
    )


def doc_index(positions, doc_ends):
    return jnp.sum((positions[:, None] >= doc_ends[None, :]).astype(jnp.int32), axis=1)


def body(tokens, norm_gain, w_query, w_key, w_value, w_out, doc_lengths):
    tok_rows = tokens.shape[0]
    col_index = lax.axis_index("col")
    row_index = lax.axis_index("row")
    query_cols = w_query.shape[1]
    local_heads = query_cols // HD
    group_size = HEADS // KVH
    kv_head = col_index * local_heads // group_size
    key_cols = lax.dynamic_slice_in_dim(w_key, kv_head * HD, HD, 1)
    value_cols = lax.dynamic_slice_in_dim(w_value, kv_head * HD, HD, 1)
    gathered = lax.all_gather(tokens, "col", axis=1, tiled=True)
    whole_f = gathered.astype(jnp.float32)
    whole_rms = lax.rsqrt(jnp.mean(whole_f * whole_f, axis=1, keepdims=True) + norm_eps)
    normed = (whole_f * whole_rms * norm_gain.astype(jnp.float32)[None, :]).astype(jnp.bfloat16)
    queries = jnp.dot(
        normed,
        lax.all_gather(w_query, "row", axis=0, tiled=True),
        preferred_element_type=jnp.float32,
    )
    keys_f = jnp.dot(
        normed,
        lax.all_gather(key_cols, "row", axis=0, tiled=True),
        preferred_element_type=jnp.float32,
    )
    values_f = jnp.dot(
        normed,
        lax.all_gather(value_cols, "row", axis=0, tiled=True),
        preferred_element_type=jnp.float32,
    )
    positions = row_index * tok_rows + jnp.arange(tok_rows, dtype=jnp.int32)
    cosine, sine = rope_tables(positions, HD)
    q_rot = rotate(queries.reshape(tok_rows, local_heads, HD), cosine, sine).astype(jnp.bfloat16)
    k_rot = (
        rotate(keys_f.reshape(tok_rows, 1, HD), cosine, sine)
        .reshape(tok_rows, HD)
        .astype(jnp.bfloat16)
    )
    v_cast = values_f.astype(jnp.bfloat16)
    doc_ends = jnp.cumsum(doc_lengths)
    query_docs = doc_index(positions, doc_ends)
    score_scale = HD ** (-0.5)
    start_state = (
        jnp.full((local_heads, tok_rows), masked_value, jnp.float32),
        jnp.zeros((local_heads, tok_rows), jnp.float32),
        jnp.zeros((local_heads, tok_rows, HD), jnp.float32),
    )
    key_piece = lax.all_gather(k_rot, "row", axis=0, tiled=True)
    value_piece = lax.all_gather(v_cast, "row", axis=0, tiled=True)
    blocks = key_piece.shape[0] // tok_rows
    key_blocks = key_piece.reshape(blocks, tok_rows, HD)
    value_blocks = value_piece.reshape(blocks, tok_rows, HD)

    def visit(state, block_in):
        key_block, value_block, block_number = block_in
        run_max, run_total, run_acc = state
        key_pos = block_number * tok_rows + jnp.arange(tok_rows, dtype=jnp.int32)
        allowed = (query_docs[:, None] == doc_index(key_pos, doc_ends)[None, :]) & (
            key_pos[None, :] <= positions[:, None]
        )
        scores = (
            jnp.einsum("qhd,kd->hqk", q_rot, key_block, preferred_element_type=jnp.float32)
            * score_scale
        )
        masked = jnp.where(allowed[None], scores, masked_value)
        new_max = jnp.maximum(run_max, jnp.max(masked, axis=2))
        factor = jnp.exp(run_max - new_max)
        weights = jnp.where(allowed[None], jnp.exp(masked - new_max[:, :, None]), 0.0)
        new_total = run_total * factor + jnp.sum(weights, axis=2)
        new_acc = run_acc * factor[:, :, None] + jnp.einsum(
            "hqk,kd->hqd",
            weights.astype(jnp.bfloat16),
            value_block,
            preferred_element_type=jnp.float32,
        )
        return ((new_max, new_total, new_acc), None)

    final_state, unused = lax.scan(
        visit, start_state, (key_blocks, value_blocks, jnp.arange(blocks, dtype=jnp.int32))
    )
    run_max, run_total, run_acc = final_state
    context = (
        (run_acc / run_total[:, :, None])
        .astype(jnp.bfloat16)
        .transpose(1, 0, 2)
        .reshape(tok_rows, query_cols)
    )
    weight_whole = lax.all_gather(w_out, "row", axis=0, tiled=True)
    projected = jnp.dot(
        lax.all_gather(context, "col", axis=1, tiled=True),
        weight_whole,
        preferred_element_type=jnp.float32,
    )
    return (tokens.astype(jnp.float32) + projected).astype(jnp.bfloat16)


def solution(mesh):
    return jax.shard_map(
        body,
        mesh=mesh,
        in_specs=(
            P("row", "col"),
            P(),
            P("row", "col"),
            P("row", None),
            P("row", None),
            P("row", "col"),
            P(),
        ),
        out_specs=P("row", "col"),
        check_vma=False,
    )
```

profile of v0, /device:TPU:0, one launch (start us, length us, event | category | flops | bytes accessed | tf_op | source)
XLA Modules:
  0.0 848.5 jit_solution(15458748518854976077)
XLA Ops:
  6.5 0.7 all-gather.8.cloned.1.call-update
  7.3 0.0 all-gather.10.cloned.1.call-start
  7.3 1.9 constant_dynamic-slice_fusion.1
  9.2 0.0 all-gather.10.cloned.1.call-update
  9.2 0.0 all-gather.14.cloned.1.call-start
  9.3 1.9 constant_dynamic-slice_fusion
  11.2 0.0 all-gather.12.cloned.1.call-start
  11.3 0.5 all-gather.12.cloned.1.call-update
  11.8 0.0 all-gather.18.cloned.1.call-start
  11.9 0.5 all-gather.18.cloned.1.call-update
  12.4 0.0 all-gather.16.cloned.1.call-start
  12.5 0.2 reduce-window.8
  12.7 1.2 multiply_cosine_fusion
  13.9 0.1 convert_reduce_fusion.1
  14.0 61.2 %all-gather.8.cloned.1.call-done = bf16[640,8192]{1,0:T(8,128)(2,1)} async-done(((bf16[640,1024]{1,0:T(8,128)(2,1)}), bf16[640,8192]{1,0:T(8,128)(2,1)}) %all-gather.8.cloned.1.call-update) | async-done | bytes 10485776 | tf_op jit(solution)/shard_map/all_gather | solution.py:46
  75.3 6.1 fusion.22
  81.4 41.4 %all-gather.10.cloned.1.call-done = bf16[8192,128]{1,0:T(8,128)(2,1)} async-done(((bf16[2048,128]{1,0:T(8,128)(2,1)}), bf16[8192,128]{1,0:T(8,128)(2,1)}) %all-gather.10.cloned.1.call-update) | async-done | bytes 2097168 | tf_op jit(solution)/shard_map/all_gather | solution.py:57
  122.8 7.8 convolution_bitcast_fusion.1
  130.6 0.7 fusion.30
  131.3 26.0 %all-gather = bf16[2560,1,128]{0,2,1:T(8,128)(2,1)S(1)} all-gather(bf16[640,1,128]{0,2,1:T(8,128)(2,1)S(1)} %pad_maximum_fusion.1), channel_id=2, replica_groups=mesh['row'=4,'col'=8] {'row'}, dimensions={0}, use_global_device_ids=true | all-gather | bytes 819200 | tf_op jit(solution)/shard_map/all_gather | solution.py:82
  157.3 0.3 copy.23
  157.7 21.4 %all-gather.14.cloned.1.call-done = bf16[8192,128]{1,0:T(8,128)(2,1)} async-done(((bf16[2048,128]{1,0:T(8,128)(2,1)}), bf16[8192,128]{1,0:T(8,128)(2,1)}) %all-gather.14.cloned.1.call-update) | async-done | bytes 2097168 | tf_op jit(solution)/shard_map/all_gather | solution.py:62
  179.1 7.5 convolution_convert_fusion
  186.6 38.9 %all_gather.29 = bf16[2560,128]{1,0:T(8,128)(2,1)} all-gather(bf16[640,128]{1,0:T(8,128)(2,1)S(1)} %convolution_convert_fusion), channel_id=1, replica_groups=mesh['row'=4,'col'=8] {'row'}, dimensions={0}, use_global_device_ids=true | all-gather | bytes 819200 | tf_op jit(solution)/shard_map/all_gather | solution.py:83
  225.4 246.9 %all-gather.12.cloned.1.call-done = bf16[8192,1024]{1,0:T(8,128)(2,1)} async-done(((bf16[2048,1024]{1,0:T(8,128)(2,1)}), bf16[8192,1024]{1,0:T(8,128)(2,1)}) %all-gather.12.cloned.1.call-update) | async-done | bytes 16777232 | tf_op jit(solution)/shard_map/all_gather | solution.py:52
  472.4 16.2 %convolution_bitcast_fusion = f32[80,8,8,128]{3,1,2,0:T(8,128)S(1)} fusion(bf16[8192,1024]{1,0:T(8,128)(2,1)} %all-gather.12.cloned.1.call-done, bf16[640,8192]{1,0:T(8,128)(2,1)} %all-gather.8.cloned.1.call-done, f32[8192]{0:T(1024)S(1)} %convert_element_type.54, f32[640]{0:T(1024)S(1)} %add_rsqrt_fusion), kind=kOutput, calls=%fused_computation.37 | convolution fusion | flops 10758389760 | bytes 29919744 | tf_op jit(solution)/shard_map/dot_general | solution.py:50
  488.6 0.6 copy.26
  489.2 0.8 fusion.37
  490.1 1.0 subtract_convert_fusion
  491.1 1.8 pad_maximum_fusion
  492.9 95.6 %while.15 = (s32[]{:T(128)}, f32[8,640]{1,0:T(8,128)S(1)}, f32[8,640]{1,0:T(8,128)S(1)}, f32[8,640,128]{2,1,0:T(8,128)}, s32[640]{0:T(1024)S(1)}, /*index=5*/s32...) while((s32[]{:T(128)}, f32[8,640]{1,0:T(8,128)S(1)}, ...), condition=%wide.region_7.8_spmd.clone, body=%wide.region_3.7_spmd.clone.sunk | while | flops 1723548800 | bytes 100618976 | solution.py:112
  492.9 0.6 dynamic_slice.39
  494.1 0.1 convert_reduce_fusion.3
  494.2 0.4 compare_and_fusion.2
  494.6 7.3 fusion.54
  501.9 8.1 fusion.55
  510.0 0.5 copy-done
  510.5 6.0 fusion.57
  516.5 0.6 dynamic_slice.39
  517.7 0.1 convert_reduce_fusion.3
  517.8 0.4 compare_and_fusion.2
  518.2 7.3 fusion.54
  525.6 8.0 fusion.55
  533.6 0.5 copy-done
  534.1 6.4 fusion.57
  540.5 0.6 dynamic_slice.39
  541.8 0.1 convert_reduce_fusion.3
  541.8 0.4 compare_and_fusion.2
  542.2 7.3 fusion.54
  549.6 8.0 fusion.55
  557.6 0.5 copy-done
  558.0 6.4 fusion.57
  564.5 0.6 dynamic_slice.39
  565.7 0.1 convert_reduce_fusion.3
  565.8 0.4 compare_and_fusion.2
  566.2 7.3 fusion.54
  573.5 8.0 fusion.55
  581.5 0.5 copy-done
  582.0 6.4 fusion.57
  588.5 2.1 copy.21
  590.6 1.3 divide_convert_fusion
  591.9 167.7 %all-gather.18.cloned.1.call-done = bf16[8192,1024]{1,0:T(8,128)(2,1)} async-done(((bf16[2048,1024]{1,0:T(8,128)(2,1)}), bf16[8192,1024]{1,0:T(8,128)(2,1)}) %all-gather.18.cloned.1.call-update) | async-done | bytes 16777232 | tf_op jit(solution)/shard_map/all_gather | solution.py:122
  759.6 63.2 %all-gather.16.cloned.1.call-done = bf16[640,8192]{0,1:T(8,128)(2,1)} async-done(((bf16[640,1024]{0,1:T(8,128)(2,1)}), bf16[640,8192]{0,1:T(8,128)(2,1)}) %all-gather.16.cloned.1.call-update) | async-done | bytes 10485776 | tf_op jit(solution)/shard_map/all_gather | solution.py:124
  822.9 18.8 %add_convert_fusion = bf16[640,1024]{1,0:T(8,128)(2,1)} fusion(bf16[640,1024]{1,0:T(8,128)(2,1)} %param.9, bf16[640,8192]{0,1:T(8,128)(2,1)} %all-gather.16.cloned.1.call-done, bf16[8192,1024]{1,0:T(8,128)(2,1)} %all-gather.18.cloned.1.call-done), kind=kOutput, calls=%fused_computation.33 | convolution fusion | flops 10739384320 | bytes 29884416 | tf_op jit(solution)/shard_map/dot_general | solution.py:123
  (37 shorter events, 0.2 us)
Async XLA Ops:
  6.5 68.7 %all-gather.8.cloned.1.call-start = ((), (), s32[]{:S(2)}) async-start(), calls=%async_computation | async-start | bytes 11796480 | tf_op jit(solution)/shard_map/all_gather | solution.py:46
  7.3 115.5 %all-gather.10.cloned.1.call-start = ((), (), s32[]{:S(2)}) async-start(), calls=%async_computation.1 | async-start | bytes 2621440 | tf_op jit(solution)/shard_map/all_gather | solution.py:57
  9.2 169.8 %all-gather.14.cloned.1.call-start = ((), (), s32[]{:S(2)}) async-start(), calls=%async_computation.3 | async-start | bytes 2621440 | tf_op jit(solution)/shard_map/all_gather | solution.py:62
  11.2 1.3 copy-start.2
  11.2 2.8 copy-start.1
  11.2 461.1 %all-gather.12.cloned.1.call-start = ((), (), s32[]{:S(2)}) async-start(), calls=%async_computation.2 | async-start | bytes 20971520 | tf_op jit(solution)/shard_map/all_gather | solution.py:52
  11.8 747.8 %all-gather.18.cloned.1.call-start = ((), (), s32[]{:S(2)}) async-start(), calls=%async_computation.5 | async-start | bytes 20971520 | tf_op jit(solution)/shard_map/all_gather | solution.py:122
  12.4 810.5 %all-gather.16.cloned.1.call-start = ((), (), s32[]{:S(2)}) async-start(), calls=%async_computation.4 | async-start | bytes 11796480 | tf_op jit(solution)/shard_map/all_gather | solution.py:124
  501.9 8.5 %copy-start = (f32[640,640,8]{1,0,2:T(8,128)S(1)}, f32[640,640,8]{1,0,2:T(8,128)}, u32[]{:S(2)}) copy-start(f32[640,640,8]{1,0,2:T(8,128)} %get-tuple-element.249) | copy-start | bytes 39321604 | tf_op jit(solution)/shard_map/while
  525.6 8.5 %copy-start = (f32[640,640,8]{1,0,2:T(8,128)S(1)}, f32[640,640,8]{1,0,2:T(8,128)}, u32[]{:S(2)}) copy-start(f32[640,640,8]{1,0,2:T(8,128)} %get-tuple-element.249) | copy-start | bytes 39321604 | tf_op jit(solution)/shard_map/while
  549.6 8.5 copy-start
  573.5 8.5 %copy-start = (f32[640,640,8]{1,0,2:T(8,128)S(1)}, f32[640,640,8]{1,0,2:T(8,128)}, u32[]{:S(2)}) copy-start(f32[640,640,8]{1,0,2:T(8,128)} %get-tuple-element.249) | copy-start | bytes 39321604 | tf_op jit(solution)/shard_map/while
Sparse Core Ops, SparseCore 0:
  9.3 65.9 all-gather.7
  76.8 45.9 all-gather.9
  124.4 54.6 all-gather.13
  180.5 291.8 all-gather.11
  473.8 285.8 all-gather.17
  761.4 61.4 all-gather.15
where the time goes:
time: 849 us; the launch traced here: 848 us
  waiting for transfers between devices  604 us (71%)
  matrix products  105 us (12%)
  blocking collectives  64.9 us (8%)
  other arithmetic  46.4 us (5%)
  between operations  13.7 us (2%)
  local copies, waits for them, and re-layouts  12 us (1%)
    all_gather x1, waiting for transfers between devices, body(): lax.all_gather(w_query, 'row', axis=0, tiled=True)  247 us
    all_gather x1, waiting for transfers between devices, body(): weight_whole = lax.all_gather(w_out, 'row', axis=0, tiled=True)  168 us
    all_gather x1, waiting for transfers between devices, body(): lax.all_gather(context, 'col', axis=1, tiled=True)  63.2 us
    all_gather x1, waiting for transfers between devices, body(): gathered = lax.all_gather(tokens, 'col', axis=1, tiled=True)  61.2 us
    all_gather x1, waiting for transfers between devices, body(): lax.all_gather(key_cols, 'row', axis=0, tiled=True)  41.4 us
    all_gather x1, blocking collectives, body(): value_piece = lax.all_gather(v_cast, 'row', axis=0, tiled=True)  38.9 us
    reduce_sum x4, other arithmetic, visit(): new_total = run_total * factor + jnp.sum(weights, axis=2)  32 us
    dot_general x4, matrix products, visit(): jnp.einsum('qhd,kd->hqk', q_rot, key_block, preferred_element_type=jnp.fl...  29.3 us
  transfers between devices with their start and end apart: 6, of which 6 were waited for; matrix products, arithmetic and copies ran while one was open for 17% of the time, Pallas kernels for 0%

commit v1 on v0

--- a/solution.py
+++ b/solution.py
@@ -79,8 +79,11 @@
         jnp.zeros((local_heads, tok_rows), jnp.float32),
         jnp.zeros((local_heads, tok_rows, HD), jnp.float32),
     )
-    key_piece = lax.all_gather(k_rot, "row", axis=0, tiled=True)
-    value_piece = lax.all_gather(v_cast, "row", axis=0, tiled=True)
+    key_piece, value_piece = jnp.split(
+        lax.all_gather(jnp.concatenate([k_rot, v_cast], axis=1), "row", axis=0, tiled=True),
+        [k_rot.shape[1]],
+        axis=1,
+    )
     blocks = key_piece.shape[0] // tok_rows
     key_blocks = key_piece.reshape(blocks, tok_rows, HD)
     value_blocks = value_piece.reshape(blocks, tok_rows, HD)

time: 849 us -> 872 us (1.027)
  waiting for transfers between devices: 604 us -> 689 us
  blocking collectives: 64.9 us -> 0 us
    all_gather x2 -> x0, blocking collectives: 64.9 us -> none  [the longest x1 38.9 us: body(): value_piece = lax.all_gather(v_cast, 'row', axis=0, tiled=True)]
    all_gather x1, waiting for transfers between devices: 247 us -> 285 us  [body(): lax.all_gather(w_query, 'row', axis=0, tiled=True)]
    all_gather x0 -> x1, waiting for transfers between devices: none -> 28.3 us  [body(): lax.all_gather(jnp.concatenate([k_rot, v_cast], axis=1), 'row', axis=0, t...]
    all_gather x1, waiting for transfers between devices: 21.4 us -> 37.6 us  [body(): lax.all_gather(value_cols, 'row', axis=0, tiled=True)]
  transfers between devices with their start and end apart: 6 -> 7, of which waited for: 6 -> 7; matrix products, arithmetic and copies ran while one was open for 17% -> 16% of each run, Pallas kernels for 0% -> 0%
where the time goes in v1:
time: 872 us
  waiting for transfers between devices  689 us (79%)
  matrix products  105 us (12%)
  other arithmetic  47.1 us (5%)
  local copies, waits for them, and re-layouts  14.4 us (2%)
  between operations  13.7 us (2%)
    all_gather x1, waiting for transfers between devices, body(): lax.all_gather(w_query, 'row', axis=0, tiled=True)  285 us
    all_gather x1, waiting for transfers between devices, body(): weight_whole = lax.all_gather(w_out, 'row', axis=0, tiled=True)  167 us
    all_gather x1, waiting for transfers between devices, body(): gathered = lax.all_gather(tokens, 'col', axis=1, tiled=True)  64 us
    all_gather x1, waiting for transfers between devices, body(): lax.all_gather(context, 'col', axis=1, tiled=True)  63.4 us
    all_gather x1, waiting for transfers between devices, body(): lax.all_gather(key_cols, 'row', axis=0, tiled=True)  41.4 us
    all_gather x1, waiting for transfers between devices, body(): lax.all_gather(value_cols, 'row', axis=0, tiled=True)  37.6 us
    reduce_sum x4, other arithmetic, visit(): new_total = run_total * factor + jnp.sum(weights, axis=2)  32 us
    dot_general x4, matrix products, visit(): jnp.einsum('qhd,kd->hqk', q_rot, key_block, preferred_element_type=jnp.fl...  29.3 us
  transfers between devices with their start and end apart: 7, of which 7 were waited for; matrix products, arithmetic and copies ran while one was open for 16% of the time, Pallas kernels for 0%

profile of v1, /device:TPU:0, one launch (start us, length us, event | category | flops | bytes accessed | tf_op | source)
XLA Modules:
  0.0 871.9 jit_solution(13127976906965144968)
XLA Ops:
  6.5 0.7 all-gather.8.cloned.1.call-update
  7.3 1.9 constant_dynamic-slice_fusion.1
  9.2 0.0 all-gather.12.cloned.1.call-start
  9.3 1.9 constant_dynamic-slice_fusion
  11.2 0.0 all-gather.14.cloned.1.call-start
  11.3 64.0 %all-gather.8.cloned.1.call-done = bf16[640,8192]{1,0:T(8,128)(2,1)} async-done(((bf16[640,1024]{1,0:T(8,128)(2,1)}), bf16[640,8192]{1,0:T(8,128)(2,1)}) %all-gather.8.cloned.1.call-update) | async-done | bytes 10485776 | tf_op jit(solution)/shard_map/all_gather | solution.py:46
  75.3 6.1 fusion.22
  81.4 41.4 %all-gather.10.cloned.1.call-done = bf16[8192,128]{1,0:T(8,128)(2,1)} async-done(((bf16[2048,128]{1,0:T(8,128)(2,1)}), bf16[8192,128]{1,0:T(8,128)(2,1)}) %all-gather.10.cloned.1.call-update) | async-done | bytes 2097168 | tf_op jit(solution)/shard_map/all_gather | solution.py:57
  122.8 7.8 convolution_bitcast_fusion.1
  130.6 0.7 fusion.30
  131.4 37.6 %all-gather.12.cloned.1.call-done = bf16[8192,128]{1,0:T(8,128)(2,1)} async-done(((bf16[2048,128]{1,0:T(8,128)(2,1)}), bf16[8192,128]{1,0:T(8,128)(2,1)}) %all-gather.12.cloned.1.call-update) | async-done | bytes 2097168 | tf_op jit(solution)/shard_map/all_gather | solution.py:62
  168.9 7.8 convolution_convert_fusion
  176.8 0.8 pad_maximum_fusion.1
  177.6 0.0 all-gather.16.cloned.1.call-start
  177.6 0.5 all-gather.16.cloned.1.call-update
  178.2 0.5 all-gather.20.cloned.1.call-update
  178.8 0.2 all-gather.18.cloned.1.call-start
  179.0 0.2 reduce-window.8
  179.2 0.1 convert_reduce_fusion.1
  179.3 1.2 multiply_cosine_fusion
  180.5 28.3 %all-gather.14.cloned.1.call-done = bf16[2560,256]{0,1:T(8,128)(2,1)} async-done(((bf16[640,256]{0,1:T(8,128)(2,1)}), bf16[2560,256]{0,1:T(8,128)(2,1)}) %all-gather.14.cloned.1.call-update) | async-done | bytes 1310736 | tf_op jit(solution)/shard_map/all_gather | solution.py:83
  208.8 1.4 fusion.38
  210.2 0.3 copy.26
  210.5 1.1 copy.27
  211.6 284.8 %all-gather.16.cloned.1.call-done = bf16[8192,1024]{1,0:T(8,128)(2,1)} async-done(((bf16[2048,1024]{1,0:T(8,128)(2,1)}), bf16[8192,1024]{1,0:T(8,128)(2,1)}) %all-gather.16.cloned.1.call-update) | async-done | bytes 16777232 | tf_op jit(solution)/shard_map/all_gather | solution.py:52
  496.5 16.3 %convolution_bitcast_fusion = f32[80,8,8,128]{3,1,2,0:T(8,128)S(1)} fusion(bf16[8192,1024]{1,0:T(8,128)(2,1)} %all-gather.16.cloned.1.call-done, bf16[640,8192]{1,0:T(8,128)(2,1)} %all-gather.8.cloned.1.call-done, f32[8192]{0:T(1024)S(1)} %convert_element_type.54, f32[640]{0:T(1024)S(1)} %add_rsqrt_fusion), kind=kOutput, calls=%fused_computation.37 | convolution fusion | flops 10758389760 | bytes 29919744 | tf_op jit(solution)/shard_map/dot_general | solution.py:50
  512.7 0.6 copy.30
  513.3 0.8 fusion.37
  514.2 1.0 subtract_convert_fusion
  515.2 1.8 pad_maximum_fusion
  517.0 95.3 %while.15 = (s32[]{:T(128)}, f32[8,640]{1,0:T(8,128)S(1)}, f32[8,640]{1,0:T(8,128)S(1)}, f32[8,640,128]{2,1,0:T(8,128)}, s32[640]{0:T(1024)S(1)}, /*index=5*/s32...) while((s32[]{:T(128)}, f32[8,640]{1,0:T(8,128)S(1)}, ...), condition=%wide.region_7.8_spmd.clone, body=%wide.region_3.7_spmd.clone.sunk | while | flops 1723548800 | bytes 100618976 | solution.py:115
  517.0 0.6 dynamic_slice.39
  518.2 0.1 convert_reduce_fusion.3
  518.2 0.4 compare_and_fusion.2
  518.6 7.3 fusion.55
  526.0 8.0 fusion.56
  534.0 0.5 copy-done
  534.5 6.0 fusion.58
  540.5 0.6 dynamic_slice.39
  541.7 0.1 convert_reduce_fusion.3
  541.8 0.4 compare_and_fusion.2
  542.2 7.3 fusion.55
  549.5 8.0 fusion.56
  557.5 0.5 copy-done
  558.0 6.4 fusion.58
  564.4 0.6 dynamic_slice.39
  565.6 0.1 convert_reduce_fusion.3
  565.7 0.4 compare_and_fusion.2
  566.1 7.3 fusion.55
  573.4 8.0 fusion.56
  581.4 0.5 copy-done
  581.9 6.4 fusion.58
  588.3 0.6 dynamic_slice.39
  589.5 0.1 convert_reduce_fusion.3
  589.6 0.4 compare_and_fusion.2
  590.0 7.3 fusion.55
  597.3 8.0 fusion.56
  605.3 0.5 copy-done
  605.8 6.4 fusion.58
  612.2 2.2 copy.24
  614.4 1.3 divide_convert_fusion
  615.7 167.2 %all-gather.20.cloned.1.call-done = bf16[8192,1024]{1,0:T(8,128)(2,1)} async-done(((bf16[2048,1024]{1,0:T(8,128)(2,1)}), bf16[8192,1024]{1,0:T(8,128)(2,1)}) %all-gather.20.cloned.1.call-update) | async-done | bytes 16777232 | tf_op jit(solution)/shard_map/all_gather | solution.py:125
  782.9 63.4 %all-gather.18.cloned.1.call-done = bf16[640,8192]{0,1:T(8,128)(2,1)} async-done(((bf16[640,1024]{0,1:T(8,128)(2,1)}), bf16[640,8192]{0,1:T(8,128)(2,1)}) %all-gather.18.cloned.1.call-update) | async-done | bytes 10485776 | tf_op jit(solution)/shard_map/all_gather | solution.py:127
  846.3 18.8 %add_convert_fusion = bf16[640,1024]{1,0:T(8,128)(2,1)} fusion(bf16[640,1024]{1,0:T(8,128)(2,1)} %param.9, bf16[640,8192]{0,1:T(8,128)(2,1)} %all-gather.18.cloned.1.call-done, bf16[8192,1024]{1,0:T(8,128)(2,1)} %all-gather.20.cloned.1.call-done), kind=kOutput, calls=%fused_computation.33 | convolution fusion | flops 10739384320 | bytes 29884416 | tf_op jit(solution)/shard_map/dot_general | solution.py:126
  (41 shorter events, 0.3 us)
Async XLA Ops:
  6.5 4.7 copy-start.1
  6.5 68.7 %all-gather.8.cloned.1.call-start = ((), (), s32[]{:S(2)}) async-start(), calls=%async_computation | async-start | bytes 11796480 | tf_op jit(solution)/shard_map/all_gather | solution.py:46
  7.3 115.5 %all-gather.10.cloned.1.call-start = ((), (), s32[]{:S(2)}) async-start(), calls=%async_computation.1 | async-start | bytes 2621440 | tf_op jit(solution)/shard_map/all_gather | solution.py:57
  9.2 159.7 %all-gather.12.cloned.1.call-start = ((), (), s32[]{:S(2)}) async-start(), calls=%async_computation.2 | async-start | bytes 2621440 | tf_op jit(solution)/shard_map/all_gather | solution.py:62
  11.2 197.6 %all-gather.14.cloned.1.call-start = ((), (), s32[]{:S(2)}) async-start(), calls=%async_computation.3 | async-start | bytes 1638400 | tf_op jit(solution)/shard_map/all_gather | solution.py:83
  177.6 1.4 copy-start.2
  177.6 318.9 %all-gather.16.cloned.1.call-start = ((), (), s32[]{:S(2)}) async-start(), calls=%async_computation.4 | async-start | bytes 20971520 | tf_op jit(solution)/shard_map/all_gather | solution.py:52
  178.2 604.7 %all-gather.20.cloned.1.call-start = ((), (), s32[]{:S(2)}) async-start(), calls=%async_computation.6 | async-start | bytes 20971520 | tf_op jit(solution)/shard_map/all_gather | solution.py:125
  178.8 667.5 %all-gather.18.cloned.1.call-start = ((), (), s32[]{:S(2)}) async-start(), calls=%async_computation.5 | async-start | bytes 11796480 | tf_op jit(solution)/shard_map/all_gather | solution.py:127
  526.0 8.5 copy-start
  549.5 8.5 copy-start
  573.4 8.5 copy-start
  597.3 8.5 copy-start
Sparse Core Ops, SparseCore 0:
  9.3 65.9 all-gather.7
  76.8 45.9 all-gather.9
  124.4 44.5 all-gather.11
  177.7 31.0 all-gather.13
  210.2 286.1 all-gather.15
  497.9 284.9 all-gather.19
  784.8 61.4 all-gather.17
